TPU v7x, 512 devices: a whole 4x8x8 slice. The times are simulated.
512 devices in a mesh: stu: 32 (over y, z_lo, core), item: 16 (over z_hi, x).
Axes of the slice: x: 4, y: 8, z: 8 (z_hi: 4, z_lo: 2; z = z_hi * 2 + z_lo), core: 2. Of those that a mesh axis runs over, the one named last changes fastest.
Arguments:
- attempts: bfloat16 [65536, 12288], P('stu', 'item'), may hold values from -0.5 to 0.5
- item_factor: bfloat16 [12288, 64], P('item'), may hold values from -0.0546875 to 0.0546875
- core_factor: float32 [64, 64], replicated, may hold values from -1 to 1.5
- student_weights: float32 [128, 64], P('stu'), may hold values from 0.3 to 3
- blocks: int32 [32, 4], P('stu'), may hold values from 1 to 8, 16 in all within a row
Outputs:
- item_mttkrp: float32 [12288, 64], P('item')
- shared_mttkrp: float32 [64, 64], replicated
- student_mttkrp: float32 [128, 64], P('stu')
Inputs may be any that keep to these rules, and one draw needn't show every extreme that they name: Each row of blocks sums to 16, and some student of each row has exactly 8 blocks.
All inputs are finite; a program needn't handle non-finite values.
Results may differ from a plain program's by a relative error of at most 0.0003.
Values sent between devices are 32-bit elements; how exact they have to be, the bound alone decides.
No kernel may reach another device: no remote copies, remote signals or barrier semaphores. Data moves between devices by JAX's collectives and lax.ppermute only.
A program may use at most 64 MiB of HBM per device.

v0:
```python
import jax
import jax.numpy as jnp
from jax import lax
from jax.sharding import PartitionSpec as P

NS_STEPS = 6
HIGHEST = lax.Precision.HIGHEST


def owner_table(counts, row_total, group_rows):
    end_rows = jnp.cumsum(counts) * 128
    start_rows = end_rows - counts * 128
    places = jnp.arange(row_total // group_rows, dtype=jnp.int32) * group_rows
    inside = (places[:, None] >= start_rows[None, :]) & (places[:, None] < end_rows[None, :])
    return inside.astype(jnp.float32)


def polar_factor(target, owners, group_rows, combine):
    row_total, width = target.shape
    blocked = target.reshape(row_total // group_rows, group_rows, width)
    identity = jnp.eye(width, dtype=jnp.float32)

    def student_gram(blocked_now):
        grams = jnp.einsum("gla,glb->gab", blocked_now, blocked_now, precision=HIGHEST)
        return combine(jnp.einsum("gk,gab->kab", owners, grams, precision=HIGHEST))

    gram_now = student_gram(blocked)
    diagonal_sum = jnp.sum(gram_now * identity, axis=(1, 2))
    inverse_norm = 1.0 / jnp.sqrt(diagonal_sum + 1e-06)
    blocked = blocked * jnp.dot(owners, inverse_norm, precision=HIGHEST)[:, None, None]
    gram_now = gram_now * (inverse_norm * inverse_norm)[:, None, None]
    for iteration in range(NS_STEPS):
        if iteration > 0:
            gram_now = student_gram(blocked)
        factor = 1.5 * identity - 0.5 * gram_now
        spread = jnp.einsum("gk,kab->gab", owners, factor, precision=HIGHEST)
        blocked = jnp.einsum("gla,gab->glb", blocked, spread, precision=HIGHEST)
    return blocked.reshape(row_total, width)


def student_cross(orthogonal, raw_sums, owners, group_rows):
    row_total, width = raw_sums.shape
    left_side = orthogonal.reshape(row_total // group_rows, group_rows, width)
    right_side = raw_sums.reshape(row_total // group_rows, group_rows, width)
    grams = jnp.einsum("gla,glb->gab", left_side, right_side, precision=HIGHEST)
    return jnp.einsum("gk,gab->kab", owners, grams, precision=HIGHEST)


def scaled_target(raw_sums, owners, group_rows, weights_here, core_factor):
    row_total, width = raw_sums.shape
    row_scale = jnp.dot(owners, weights_here, precision=HIGHEST)
    scaled = raw_sums.reshape(row_total // group_rows, group_rows, width) * row_scale[:, None, :]
    return jnp.dot(scaled.reshape(row_total, width), core_factor.T, precision=HIGHEST)


def local(attempts, item_factor, core_factor, student_weights, blocks):
    row_total = attempts.shape[0]
    width = item_factor.shape[1]
    counts = blocks[0]
    full_owners = owner_table(counts, row_total, 128)
    local_sums = jnp.dot(attempts, item_factor, preferred_element_type=jnp.float32)
    raw_sums = lax.psum(local_sums, "item")
    target = scaled_target(raw_sums, full_owners, 128, student_weights, core_factor)
    orthogonal = polar_factor(target, full_owners, 128, lambda summand: summand)
    crossed = student_cross(orthogonal, raw_sums, full_owners, 128)
    row_scale = jnp.dot(full_owners, student_weights, precision=HIGHEST)
    lifted = jnp.dot(orthogonal, core_factor, precision=HIGHEST)
    lifted = lifted.reshape(row_total // 128, 128, width) * row_scale[:, None, :]
    weighted = lifted.reshape(row_total, width).astype(jnp.bfloat16)
    item_part = lax.dot_general(
        attempts, weighted, (((0,), (0,)), ((), ())), preferred_element_type=jnp.float32
    )
    shared_part = jnp.einsum("kab,kb->ab", crossed, student_weights, precision=HIGHEST)
    student_part = jnp.einsum("ab,kab->kb", core_factor, crossed, precision=HIGHEST)
    item_total, shared_total = lax.psum((item_part, shared_part), "stu")
    return (item_total, shared_total, student_part)


def solution(mesh):
    in_specs = (P("stu", "item"), P("item", None), P(), P("stu", None), P("stu", None))
    out_specs = (P("item", None), P(), P("stu", None))
    return jax.shard_map(local, mesh=mesh, in_specs=in_specs, out_specs=out_specs, check_vma=False)
```

profile of v0, /device:TPU:2, one launch (start us, length us, event | category | flops | bytes accessed | tf_op | source)
XLA Modules:
  0.0 437.9 jit_solution(16412960263734139279)
XLA Ops:
  7.2 0.0 copy-start
  7.2 0.0 all-reduce.3.cloned.1.call-start
  7.3 1.8 copy-done
  9.1 2.8 fusion.73
  11.8 0.0 all-reduce.3.cloned.1.call-update
  11.9 0.0 all-reduce.5.cloned.1.call-start
  11.9 0.2 reduce-window.4
  12.1 0.1 compare_and_fusion
  12.2 0.2 fusion.74
  12.4 0.1 copy.43
  12.5 176.2 %all-reduce.3.cloned.1.call-done = f32[2048,64]{0,1:T(8,128)} async-done(((f32[2048,64]{0,1:T(8,128)}), f32[2048,64]{0,1:T(8,128)}) %all-reduce.3.cloned.1.call-update) | async-done | bytes 524304 | tf_op jit(solution)/shard_map/psum | solution.py:62
  188.7 0.2 mul.120.clone
  188.9 1.8 fusion.11
  190.8 0.9 fusion.75
  191.7 0.8 multiply_reduce_fusion.2
  192.5 0.1 convolution_bitcast_fusion.1
  192.6 0.5 fusion.39
  193.1 1.1 fusion.31
  194.2 0.9 fusion.76
  195.2 0.6 fusion.6
  195.8 0.5 fusion.63
  196.3 1.1 fusion.28
  197.4 0.9 fusion.77
  198.3 0.6 fusion.5
  198.9 0.5 fusion.60
  199.4 1.1 fusion.25
  200.5 0.9 fusion.78
  201.4 0.6 fusion.4
  202.0 0.5 fusion.57
  202.5 1.3 fusion.22
  203.8 0.9 fusion.79
  204.7 0.6 fusion.3
  205.3 0.5 fusion.54
  205.8 1.1 fusion.19
  206.9 0.9 fusion.80
  207.8 0.6 fusion.2
  208.5 0.5 fusion.51
  208.9 1.1 fusion.16
  210.0 0.8 copy-done.1
  210.8 0.6 fusion.1
  211.4 1.3 convolution_bitcast_fusion
  212.8 0.0 all-reduce.5.cloned.1.call-update
  212.8 2.1 fusion.8
  215.0 0.7 multiply_reduce_fusion.1
  215.6 104.4 %psum.23 = f32[64,64]{1,0:T(8,128)} all-reduce(f32[64,64]{1,0:T(8,128)S(1)} %bitcast.121), channel_id=1, replica_groups=mesh['stu'=32,'item'=16] {'stu'}, use_global_device_ids=true, to_apply=%region_4.5 | all-reduce | flops 4096 | bytes 32768 | tf_op jit(solution)/shard_map/psum | solution.py:75
  320.1 0.7 multiply_reduce_fusion
  320.7 108.8 %all-reduce.5.cloned.1.call-done = f32[768,64]{0,1:T(8,128)} async-done(((f32[768,64]{0,1:T(8,128)}), f32[768,64]{0,1:T(8,128)}) %all-reduce.5.cloned.1.call-update) | async-done | bytes 196624 | tf_op jit(solution)/shard_map/psum | solution.py:75
  429.5 1.6 copy.97
  (13 shorter events, 0.1 us)
Async XLA Ops:
  7.2 1.9 copy-start
  7.2 4.7 %copy-start.4 = (s32[1,4]{1,0:T(1,128)S(1)}, s32[1,4]{1,0:T(1,128)}, u32[]{:S(2)}) copy-start(s32[1,4]{1,0:T(1,128)} %param.9) | copy-start | bytes 52
  7.2 5.0 %copy-start.3 = (f32[4,64]{1,0:T(4,128)S(1)}, f32[4,64]{1,0:T(4,128)}, u32[]{:S(2)}) copy-start(f32[4,64]{1,0:T(4,128)} %param.8) | copy-start | bytes 3076
  7.2 181.7 %copy-start.2 = (f32[64,64]{1,0:T(8,128)S(1)}, f32[64,64]{1,0:T(8,128)}, u32[]{:S(2)}) copy-start(f32[64,64]{1,0:T(8,128)} %param.7) | copy-start | bytes 49156
  7.2 181.5 %all-reduce.3.cloned.1.call-start = ((), (), s32[]{:S(2)}) async-start(), calls=%async_computation | async-start | bytes 1048576 | tf_op jit(solution)/shard_map/psum | solution.py:62
  11.9 417.6 %all-reduce.5.cloned.1.call-start = ((), (), s32[]{:S(2)}) async-start(), calls=%async_computation.1 | async-start | bytes 393216 | tf_op jit(solution)/shard_map/psum | solution.py:75
  210.0 0.8 copy-start.1
Sparse Core Ops, SparseCore 0:
  12.0 176.7 all-reduce.2
  212.9 216.5 all-reduce.4
where the time goes:
time: 438 us
  waiting for transfers between devices  285 us (65%)
  blocking collectives  104 us (24%)
  matrix products  28.7 us (7%)
  between operations  14.3 us (3%)
  local copies, waits for them, and re-layouts  4.52 us (1%)
    psum x1, waiting for transfers between devices, local(): raw_sums = lax.psum(local_sums, 'item')  176 us
    psum x1, waiting for transfers between devices, local(): item_total, shared_total = lax.psum((item_part, shared_part), 'stu')  109 us
    psum x1, blocking collectives, local(): item_total, shared_total = lax.psum((item_part, shared_part), 'stu')  104 us
  transfers between devices with their start and end apart: 2, of which 2 were waited for; matrix products, arithmetic and copies ran while one was open for 1% of the time, Pallas kernels for 0%

commit v1 on v0

--- a/solution.py
+++ b/solution.py
@@ -54,12 +54,18 @@
 
 
 def local(attempts, item_factor, core_factor, student_weights, blocks):
+
+    def rates_pass(buf):
+        opened = lax.all_gather(buf, "item")
+        r_now = jnp.sum(opened, 0)
+        return r_now
+
     row_total = attempts.shape[0]
     width = item_factor.shape[1]
     counts = blocks[0]
     full_owners = owner_table(counts, row_total, 128)
     local_sums = jnp.dot(attempts, item_factor, preferred_element_type=jnp.float32)
-    raw_sums = lax.psum(local_sums, "item")
+    raw_sums = rates_pass(local_sums)
     target = scaled_target(raw_sums, full_owners, 128, student_weights, core_factor)
     orthogonal = polar_factor(target, full_owners, 128, lambda summand: summand)
     crossed = student_cross(orthogonal, raw_sums, full_owners, 128)

time: 438 us -> 399 us (0.911)
  waiting for transfers between devices: 285 us -> 234 us
  local copies, waits for them, and re-layouts: 4.52 us -> 11.6 us
    psum x1 -> x0, waiting for transfers between devices: 176 us -> none  [local(): raw_sums = lax.psum(local_sums, 'item')]
    all_gather x0 -> x1, waiting for transfers between devices: none -> 128 us  [rates_pass(): opened = lax.all_gather(buf, 'item')]
    unnamed x12 -> x10, local copies, waits for them, and re-layouts: 4.33 us -> 11.6 us
where the time goes in v1:
time: 399 us
  waiting for transfers between devices  234 us (59%)
  blocking collectives  107 us (27%)
  matrix products  28.4 us (7%)
  between operations  14.2 us (4%)
  local copies, waits for them, and re-layouts  11.6 us (3%)
    all_gather x1, waiting for transfers between devices, rates_pass(): opened = lax.all_gather(buf, 'item')  128 us
    psum x1, blocking collectives, local(): item_total, shared_total = lax.psum((item_part, shared_part), 'stu')  107 us
    psum x1, waiting for transfers between devices, local(): item_total, shared_total = lax.psum((item_part, shared_part), 'stu')  106 us
    unnamed x10, local copies, waits for them, and re-layouts  11.6 us
  transfers between devices with their start and end apart: 2, of which 2 were waited for; matrix products, arithmetic and copies ran while one was open for 1% of the time, Pallas kernels for 0%

profile of v1, /device:TPU:2, one launch (start us, length us, event | category | flops | bytes accessed | tf_op | source)
XLA Modules:
  0.0 398.5 jit_solution(12385973965452160905)
XLA Ops:
  7.2 0.0 copy-start
  7.2 0.0 all-gather.3.cloned.1.call-start
  7.2 1.8 copy-done
  9.1 2.8 fusion.72
  11.9 0.0 all-gather.3.cloned.1.call-update
  11.9 0.0 all-reduce.2.cloned.1.call-start
  11.9 0.2 reduce-window.4
  12.2 0.1 compare_and_fusion
  12.3 0.2 fusion.73
  12.4 127.9 %all-gather.3.cloned.1.call-done = f32[32768,64]{0,1:T(8,128)} async-done(((f32[2048,64]{0,1:T(8,128)}), f32[32768,64]{0,1:T(8,128)}) %all-gather.3.cloned.1.call-update) | async-done | bytes 8388624 | tf_op jit(solution)/shard_map/all_gather | solution.py:59
  140.4 8.1 %copy.43 = f32[8,8,16,2048]{3,2,1,0:T(8,128)S(1)} copy(f32[8,8,16,2048]{3,1,2,0:T(8,128)} %bitcast.113) | data formatting | bytes 16777216
  148.5 0.0 copy-start.1
  148.5 1.7 bitcast_reduce_fusion
  150.2 0.7 fusion.9
  151.0 0.9 fusion.74
  151.9 0.8 multiply_reduce_fusion.2
  152.7 0.1 convolution_bitcast_fusion.1
  152.8 0.5 fusion.38
  153.3 1.1 fusion.27
  154.4 0.9 fusion.75
  155.4 0.6 fusion.6
  156.0 0.7 fusion.62
  156.6 1.1 fusion.24
  157.7 0.9 fusion.76
  158.7 0.6 fusion.5
  159.3 0.5 fusion.59
  159.8 1.1 fusion.21
  160.9 0.9 fusion.77
  161.8 0.6 fusion.4
  162.4 0.5 fusion.56
  162.9 1.1 fusion.18
  164.0 0.9 fusion.78
  164.9 0.6 fusion.3
  165.5 0.5 fusion.53
  166.0 1.1 fusion.15
  167.1 0.9 fusion.79
  168.0 0.6 fusion.2
  168.7 0.5 fusion.50
  169.1 1.3 fusion.12
  170.4 1.7 fusion.7
  172.2 0.6 fusion.1
  172.8 1.3 convolution_bitcast_fusion
  174.1 0.0 all-reduce.2.cloned.1.call-update
  174.2 1.7 multiply_reduce_fusion.1
  175.8 107.2 %psum.15 = f32[64,64]{1,0:T(8,128)} all-reduce(f32[64,64]{1,0:T(8,128)S(1)} %bitcast.115), channel_id=1, replica_groups=mesh['stu'=32,'item'=16] {'stu'}, use_global_device_ids=true, to_apply=%region_4.5 | all-reduce | flops 4096 | bytes 32768 | tf_op jit(solution)/shard_map/psum | solution.py:81
  283.0 0.7 multiply_reduce_fusion
  283.7 106.4 %all-reduce.2.cloned.1.call-done = f32[768,64]{0,1:T(8,128)} async-done(((f32[768,64]{0,1:T(8,128)}), f32[768,64]{0,1:T(8,128)}) %all-reduce.2.cloned.1.call-update) | async-done | bytes 196624 | tf_op jit(solution)/shard_map/psum | solution.py:81
  390.1 1.6 copy.87
  (11 shorter events, 0.0 us)
Async XLA Ops:
  7.2 1.9 copy-start
  7.2 4.8 %copy-start.3 = (s32[1,4]{1,0:T(1,128)S(1)}, s32[1,4]{1,0:T(1,128)}, u32[]{:S(2)}) copy-start(s32[1,4]{1,0:T(1,128)} %param.9) | copy-start | bytes 52
  7.2 5.1 %copy-start.2 = (f32[4,64]{1,0:T(4,128)S(1)}, f32[4,64]{1,0:T(4,128)}, u32[]{:S(2)}) copy-start(f32[4,64]{1,0:T(4,128)} %param.8) | copy-start | bytes 3076
  7.2 133.2 %all-gather.3.cloned.1.call-start = ((), (), s32[]{:S(2)}) async-start(), calls=%async_computation.1 | async-start | bytes 8912896 | tf_op jit(solution)/shard_map/all_gather | solution.py:59
  11.9 378.2 %all-reduce.2.cloned.1.call-start = ((), (), s32[]{:S(2)}) async-start(), calls=%async_computation | async-start | bytes 393216 | tf_op jit(solution)/shard_map/psum | solution.py:81
  148.5 1.7 copy-start.1
Sparse Core Ops, SparseCore 0:
  12.0 128.3 all-gather.2
  174.3 215.7 all-reduce.1
